TPU v7x, 512 devices: a whole 4x8x8 slice. The times are simulated.
512 devices in a mesh: pw: 8 (over x, y_lo), pair: 64 (over y_hi, z, core).
Axes of the slice: x: 4, y: 8 (y_hi: 4, y_lo: 2; y = y_hi * 2 + y_lo), z: 8, core: 2. Of those that a mesh axis runs over, the one named last changes fastest.
Arguments:
- valence_pairs: bfloat16 [64, 64, 8192], P('pair', None, 'pw'), may hold values from -0.59765625 to 0.59765625
- conduction_pairs: bfloat16 [64, 256, 8192], P('pair', None, 'pw'), may hold values from -0.59765625 to 0.59765625
- screening: float32 [8192], P('pw'), may hold values from 0.1 to 2
Outputs:
- kernel: float32 [64, 64, 64, 256], P('pair', None, 'pw')
All inputs are finite; a program needn't handle non-finite values.
Results may differ from a plain program's by a relative error of at most 0.0029.
Values may be sent and summed in bfloat16 or wider, within the bound.
No kernel may reach another device: no remote copies, remote signals or barrier semaphores. Data moves between devices by JAX's collectives and lax.ppermute only.
A program may use at most 64 MiB of HBM per device.

v0:
```python
import jax
import jax.numpy as jnp
from jax import lax
from jax.sharding import PartitionSpec as P


def split_up(shard, dim, devices):
    before, after = (shard.shape[:dim], shard.shape[dim + 1 :])
    return jnp.moveaxis(shard.reshape(*before, devices, -1, *after), dim, 0)


def sent_and_summed(shard, axis, dim):
    parts = split_up(shard, dim, lax.axis_size(axis))
    arrived = lax.all_to_all(parts, axis, split_axis=0, concat_axis=0, tiled=True)
    return arrived.sum(axis=0)


def contract(piece, flat_right, band_dev, conduction):
    first, second, width = piece.shape
    product = lax.dot_general(
        piece.reshape(first * second, width),
        flat_right,
        (((1,), (1,)), ((), ())),
        preferred_element_type=jnp.float32,
    )
    return product.reshape(first, second, band_dev, conduction)


def route_rows(terms):
    owned = lax.all_to_all(terms, "pair", split_axis=0, concat_axis=2, tiled=True)
    return owned.transpose(0, 2, 1, 3)


def body(valence_pairs, conduction_pairs, screening):
    screened = (valence_pairs.astype(jnp.float32) * screening[None, None, :]).astype(jnp.bfloat16)
    band_dev, conduction, plane_dev = conduction_pairs.shape
    flat_local = conduction_pairs.reshape(band_dev * conduction, plane_dev)
    partial_value = contract(
        lax.all_gather(screened, "pair", axis=0, tiled=True), flat_local, band_dev, conduction
    )
    terms = sent_and_summed(partial_value, "pw", 1)
    return route_rows(terms)


def solution(mesh):
    placed = (P("pair", None, "pw"), P("pair", None, "pw"), P("pw"))
    return jax.shard_map(
        body, mesh=mesh, in_specs=placed, out_specs=P("pair", None, "pw", None), check_vma=False
    )
```

profile of v0, /device:TPU:1, one launch (start us, length us, event | category | flops | bytes accessed | tf_op | source)
XLA Modules:
  0.0 217.4 jit_solution(5464466841965984867)
XLA Ops:
  6.5 0.0 copy-start
  6.5 0.0 all-gather.2.cloned.1.call-start
  6.5 1.6 multiply_convert_fusion
  8.2 0.0 all-gather.2.cloned.1.call-update
  8.2 112.5 %all-gather.2.cloned.1.call-done = bf16[64,64,1024]{2,1,0:T(8,128)(2,1)} async-done(((bf16[1,64,1024]{2,1,0:T(8,128)(2,1)}), bf16[64,64,1024]{2,1,0:T(8,128)(2,1)}) %all-gather.2.cloned.1.call-update) | async-done | bytes 8388624 | tf_op jit(solution)/shard_map/all_gather | solution.py:39
  120.7 0.0 copy-done
  120.7 5.7 %fusion.2 = f32[8,64,8,1,256]{4,2,0,1,3:T(8,128)S(1)} fusion(bf16[64,64,1024]{2,1,0:T(8,128)(2,1)} %all-gather.2.cloned.1.call-done, bf16[1,256,1024]{2,1,0:T(8,128)(2,1)S(1)} %copy-done), kind=kOutput, calls=%fused_computation.2 | convolution fusion | flops 2147483648 | bytes 13107200 | tf_op jit(solution)/shard_map/dot_general | solution.py:20
  126.5 0.4 copy.4
  126.9 52.5 %all_to_all.23 = f32[8,64,8,1,256]{4,2,1,3,0:T(8,128)} all-to-all(f32[8,64,8,1,256]{4,2,1,3,0:T(8,128)S(1)} %copy.4), channel_id=1, replica_groups=mesh['pw'=8,'pair'=64] {'pw'}, dimensions={0} | all-to-all | bytes 8388608 | tf_op jit(solution)/shard_map/all_to_all | solution.py:14
  179.4 2.5 %reduce_sum.11 = f32[64,8,256]{2,1,0:T(8,128)S(1)} reduce(f32[8,64,8,1,256]{4,2,1,3,0:T(8,128)} %all_to_all.23, f32[]{:T(128)} %constant.0.clone.1), dimensions={0,3}, to_apply=%region_0.0 | reduce | flops 917504 | bytes 4718596 | tf_op jit(solution)/shard_map/reduce_sum | solution.py:15
  182.0 27.8 %all_to_all.24 = f32[64,8,1,256]{3,1,2,0:T(8,128)S(1)} all-to-all(f32[64,8,1,256]{3,1,2,0:T(8,128)S(1)} %bitcast.24), channel_id=1, replica_groups=mesh['pw'=8,'pair'=64] {'pair'}, dimensions={0} | all-to-all | bytes 1048576 | tf_op jit(solution)/shard_map/all_to_all | solution.py:30
  209.8 0.8 copy.7
Async XLA Ops:
  6.5 114.2 %copy-start = (bf16[1,256,1024]{2,1,0:T(8,128)(2,1)S(1)}, bf16[1,256,1024]{2,1,0:T(8,128)(2,1)}, u32[]{:S(2)}) copy-start(bf16[1,256,1024]{2,1,0:T(8,128)(2,1)} %param.4) | copy-start | bytes 1572868
  6.5 114.2 %all-gather.2.cloned.1.call-start = ((), (), s32[]{:S(2)}) async-start(), calls=%async_computation.2 | async-start | bytes 8519680 | tf_op jit(solution)/shard_map/all_gather | solution.py:39
Sparse Core Ops, SparseCore 0:
  10.7 109.9 all-gather.1
where the time goes:
time: 218 us; the launch traced here: 217 us
  waiting for transfers between devices  113 us (52%)
  blocking collectives  80.3 us (37%)
  between operations  13.4 us (6%)
  matrix products  5.75 us (3%)
  other arithmetic  4.16 us (2%)
    all_gather x1, waiting for transfers between devices, body(): lax.all_gather(screened, 'pair', axis=0, tiled=True)  113 us
    all_to_all x1, blocking collectives, sent_and_summed(): lax.all_to_all(parts, axis, split_axis=0, concat_axis=0, tiled=True)  52.5 us
    all_to_all x1, blocking collectives, route_rows(): lax.all_to_all(terms, 'pair', split_axis=0, concat_axis=2, tiled=True)  27.8 us
    dot_general x1, matrix products, contract(): lax.dot_general(piece.reshape(first * second, width), flat_right, (((1,),...  5.75 us
  transfers between devices with their start and end apart: 1, of which 1 were waited for; matrix products, arithmetic and copies ran while one was open for 0% of the time, Pallas kernels for 0%

commit v1 on v0

--- a/solution.py
+++ b/solution.py
@@ -36,7 +36,12 @@
     band_dev, conduction, plane_dev = conduction_pairs.shape
     flat_local = conduction_pairs.reshape(band_dev * conduction, plane_dev)
     partial_value = contract(
-        lax.all_gather(screened, "pair", axis=0, tiled=True), flat_local, band_dev, conduction
+        jnp.concatenate(
+            lax.all_to_all(jnp.stack([screened] * lax.axis_size("pair")), "pair", 0, 0), axis=0
+        ),
+        flat_local,
+        band_dev,
+        conduction,
     )
     terms = sent_and_summed(partial_value, "pw", 1)
     return route_rows(terms)

time: 218 us -> 322 us (1.48)
  blocking collectives: 80.3 us -> 313 us
  waiting for transfers between devices: 113 us -> 0 us
  between operations: 13.4 us -> 0.03 us
  matrix products: 5.75 us -> 2.47 us
    all_to_all x0 -> x1, blocking collectives: none -> 226 us  [body(): lax.all_to_all(jnp.stack([screened] * lax.axis_size('pair')), 'pair', 0, 0)]
    all_gather x1 -> x0, waiting for transfers between devices: 113 us -> none  [body(): lax.all_gather(screened, 'pair', axis=0, tiled=True)]
    all_to_all x1, blocking collectives: 27.8 us -> 34.9 us  [route_rows(): lax.all_to_all(terms, 'pair', split_axis=0, concat_axis=2, tiled=True)]
    dot_general x1, matrix products: 5.75 us -> 2.47 us  [contract(): lax.dot_general(piece.reshape(first * second, width), flat_right, (((1,),...]
  transfers between devices with their start and end apart: 1 -> 0, of which waited for: 1 -> 0; matrix products, arithmetic and copies ran while one was open for 0% -> 0% of each run, Pallas kernels for 0% -> 0%
where the time goes in v1:
time: 322 us
  blocking collectives  313 us (97%)
  other arithmetic  3.51 us (1%)
    all_to_all x1, blocking collectives, body(): lax.all_to_all(jnp.stack([screened] * lax.axis_size('pair')), 'pair', 0, 0)  226 us
    all_to_all x1, blocking collectives, sent_and_summed(): lax.all_to_all(parts, axis, split_axis=0, concat_axis=0, tiled=True)  52.2 us
    all_to_all x1, blocking collectives, route_rows(): lax.all_to_all(terms, 'pair', split_axis=0, concat_axis=2, tiled=True)  34.9 us

profile of v1, /device:TPU:1, one launch (start us, length us, event | category | flops | bytes accessed | tf_op | source)
XLA Modules:
  0.0 321.7 jit_solution(17929188492911294838)
XLA Ops:
  0.0 0.0 copy-start
  0.0 1.0 fusion.6
  1.0 1.1 stack.2
  2.1 226.4 %all_to_all.28 = bf16[64,1,64,1024]{3,2,1,0:T(8,128)(2,1)S(1)} all-to-all(bf16[64,1,64,1024]{3,2,1,0:T(8,128)(2,1)S(1)} %stack.2), channel_id=1, replica_groups=mesh['pw'=8,'pair'=64] {'pair'}, dimensions={0} | all-to-all | bytes 16777216 | tf_op jit(solution)/shard_map/all_to_all | solution.py:40
  228.4 0.0 copy-done
  228.4 2.5 fusion.2
  230.9 0.4 copy.4
  231.3 52.2 %all_to_all.29 = f32[8,64,8,1,256]{4,2,1,3,0:T(8,128)} all-to-all(f32[8,64,8,1,256]{4,2,1,3,0:T(8,128)S(1)} %copy.4), channel_id=1, replica_groups=mesh['pw'=8,'pair'=64] {'pw'}, dimensions={0} | all-to-all | bytes 8388608 | tf_op jit(solution)/shard_map/all_to_all | solution.py:14
  283.5 2.5 reduce_sum.11
  286.1 34.9 %all_to_all.30 = f32[64,8,1,256]{3,1,2,0:T(8,128)S(1)} all-to-all(f32[64,8,1,256]{3,1,2,0:T(8,128)S(1)} %bitcast.26), channel_id=1, replica_groups=mesh['pw'=8,'pair'=64] {'pair'}, dimensions={0} | all-to-all | bytes 1048576 | tf_op jit(solution)/shard_map/all_to_all | solution.py:30
  320.9 0.8 copy.7
Async XLA Ops:
  0.0 228.4 %copy-start = (bf16[1,256,1024]{2,1,0:T(8,128)(2,1)S(1)}, bf16[1,256,1024]{2,1,0:T(8,128)(2,1)}, u32[]{:S(2)}) copy-start(bf16[1,256,1024]{2,1,0:T(8,128)(2,1)} %param.4) | copy-start | bytes 1572868
